TPU v7x, 128 devices: a whole 4x4x4 slice. The times are simulated.
128 devices in a mesh: seq: 8 (over x_hi, z), res: 16 (over x_lo, y, core).
Axes of the slice: x: 4 (x_hi: 2, x_lo: 2; x = x_hi * 2 + x_lo), y: 4, z: 4, core: 2. Of those that a mesh axis runs over, the one named last changes fastest.
Arguments:
- alignment: bfloat16 [32, 768, 768], P('seq', 'res'), may hold values from -6 to 6
- cotangent: bfloat16 [32, 768, 768], P('seq', 'res'), may hold values from -6 to 6
- gain_row: float32 [768], replicated, may hold values from 0.25 to 1.75
- query_row: bfloat16 [768, 768], replicated, may hold values from -0.25 to 0.25
- key_row: bfloat16 [768, 768], replicated, may hold values from -1.2 to 1.2
- value_row: bfloat16 [768, 768], replicated, may hold values from -0.21875 to 0.21875
- out_row: bfloat16 [768, 768], replicated, may hold values from -0.21875 to 0.21875
- gain_col: float32 [768], replicated, may hold values from 0.25 to 1.75
- query_col: bfloat16 [768, 768], replicated, may hold values from -0.25 to 0.25
- key_col: bfloat16 [768, 768], replicated, may hold values from -3.6 to 3.6
- value_col: bfloat16 [768, 768], replicated, may hold values from -0.21875 to 0.21875
- out_col: bfloat16 [768, 768], replicated, may hold values from -0.21875 to 0.21875
Outputs:
- block_out: bfloat16 [32, 768, 768], P('seq', 'res')
- input_grad: bfloat16 [32, 768, 768], P('seq', 'res')
All inputs are finite; a program needn't handle non-finite values.
Results may differ from a plain program's by a relative error of at most 0.02.
Values may be sent and summed in bfloat16 or wider, within the bound.
No kernel may reach another device: no remote copies, remote signals or barrier semaphores. Data moves between devices by JAX's collectives and lax.ppermute only.
A program may use at most 192 MiB of HBM per device.

v0:
```python
import math

import jax
import jax.numpy as jnp
from jax import lax
from jax.experimental import pallas as pl
from jax.experimental.pallas import tpu as pltpu
from jax.sharding import Mesh
from jax.sharding import PartitionSpec as P

F32 = jnp.float32
BF16 = jnp.bfloat16
D = 768
HEADS = 12
HEAD_DIM = 64
SEQ = ("xh", "z")
GRP = ("xl", "c")
WIDE = ("xh", "z", "xl", "c")
ALLRES = ("y", "xl", "c")
NS, NG, NY = 8, 4, 4
GH = HEADS // NG
S = 4
R = 48
I = R * NG
CR = 6
CP = 8
TOK = NS * S * CP
ROWS = GH * I // NS
SENT = S * CR
BLOCK = ROWS + 2 * SENT
WIDTH = GH * S * HEAD_DIM
ROW_SCALE = 1.0 / math.sqrt(HEAD_DIM * 32)
COL_SCALE = 1.0 / math.sqrt(HEAD_DIM)


def dot(a, b):
    return lax.dot_general(a, b, (((1,), (0,)), ((), ())), preferred_element_type=F32)


def dot_nt(a, b):
    return lax.dot_general(a, b, (((1,), (1,)), ((), ())), preferred_element_type=F32)


def dot_tn(a, b):
    return lax.dot_general(a, b, (((0,), (0,)), ((), ())), preferred_element_type=F32)


def call(kernel, outs, *args, mem=16, scratch=(), far=(), sems=0, cost=None):
    scratch = list(scratch)
    if sems:
        scratch.append(pltpu.SemaphoreType.DMA((sems,)))
    args = [
        pltpu.with_memory_space_constraint(a, pltpu.HBM) if i in far else a
        for i, a in enumerate(args)
    ]
    shapes = [jax.ShapeDtypeStruct(*o) if isinstance(o, tuple) else o for o in outs]
    spaces = [pltpu.VMEM if isinstance(o, tuple) else o.memory_space for o in outs]
    res = pl.pallas_call(
        kernel,
        out_shape=shapes,
        in_specs=[
            pl.BlockSpec(memory_space=pltpu.HBM if i in far else pltpu.VMEM)
            for i in range(len(args))
        ],
        out_specs=[pl.BlockSpec(memory_space=m) for m in spaces],
        scratch_shapes=scratch,
        cost_estimate=cost,
        compiler_params=pltpu.CompilerParams(vmem_limit_bytes=mem * 2**20),
    )(*args)
    return res[0] if len(outs) == 1 else res


def fetch(sources, targets, sems, wait_only=False, cuts=1):
    reads, at = [], 0
    for src, dst in zip(sources, targets):
        copies = []
        parts = cuts if src.shape[0] == D and len(src.shape) == 2 else 1
        for n in range(parts):
            rows = slice(n * D // parts, (n + 1) * D // parts)
            a, b = (src.at[rows], dst.at[rows]) if parts > 1 else (src, dst)
            copies.append(pltpu.make_async_copy(a, b, sems.at[at]))
            at += 1
        for c in copies:
            c.start()

        def read(copies=copies, dst=dst):
            for c in copies:
                c.wait()
            copies.clear()
            return None if wait_only else dst[...]

        reads.append(read)
    return reads


class Pushes:
    def __init__(self, sems, first=0):
        self.sems, self.first, self.begun = sems, first, []

    def start(self, src, dst):
        c = pltpu.make_async_copy(src, dst, self.sems.at[self.first + len(self.begun)])
        c.start()
        self.begun.append(c)

    def finish(self):
        for c in self.begun:
            c.wait()


def my_group():
    return lax.axis_index("xl") * 2 + lax.axis_index("c")


def halves(a, b, half_a, half_b):
    low = lax.broadcasted_iota(jnp.int32, a.shape, 1) < 64
    a = a if half_a == 0 else pltpu.roll(a, 64, 1)
    b = b if half_b == 1 else pltpu.roll(b, 64, 1)
    return jnp.where(low, a, b)


def blk(v, n):
    return v[:, n * 128 : (n + 1) * 128]


def to_column():
    row = lax.broadcasted_iota(jnp.int32, (S * R, S * R), 0)
    col = lax.broadcasted_iota(jnp.int32, (S * R, S * R), 1)
    want = ((row // CR) % S) * R + (row // (CR * S)) * CR + row % CR
    return jnp.where(col == want, 1.0, 0.0).astype(BF16)


def to_padded():
    row = lax.broadcasted_iota(jnp.int32, (TOK, S * R), 0)
    col = lax.broadcasted_iota(jnp.int32, (TOK, S * R), 1)
    r = row % CP
    return jnp.where((r < CR) & (col == (row // CP) * CR + r), 1.0, 0.0).astype(BF16)


def to_wide():
    row = lax.broadcasted_iota(jnp.int32, (TOK, I), 0)
    col = lax.broadcasted_iota(jnp.int32, (TOK, I), 1)
    r = row % CP
    want = ((row // CP) % NG) * R + (row // (CP * NG)) * CR + r
    return jnp.where((r < CR) & (col == want), 1.0, 0.0).astype(BF16)


def moments(v):
    mean = jnp.mean(v, axis=-1, keepdims=True)
    centred = v - mean
    r = lax.rsqrt(jnp.mean(centred * centred, axis=-1, keepdims=True) + 1e-05)
    return centred * r, r


def norm_grad(grad, gain, hat, r):
    g = grad * gain
    return r * (
        g - jnp.mean(g, axis=-1, keepdims=True) - hat * jnp.mean(g * hat, axis=-1, keepdims=True)
    )


def pieces(y, put, after=None):
    for g in range(NG):
        for h in range(GH):
            n = g * GH + h
            src = blk(y, n // 2)
            for sp in range(2):
                a = src[2 * sp * R : (2 * sp + 1) * R]
                b = src[(2 * sp + 1) * R : (2 * sp + 2) * R]
                put(g, h * 256 + sp * 128, halves(a, b, n % 2, n % 2).astype(BF16))
        if after is not None:
            after(g)


def normed_input(x, gain):
    hat, _ = moments(x.astype(F32).reshape(S * R, D))
    return (hat * gain.reshape(1, D)).astype(BF16)


def k_keys(x, gain, w, keys, x_s, g_s, w_s, keys_s, sems):
    x, gain, w = fetch((x, gain, w), (x_s, g_s, w_s), sems, cuts=4)
    push = Pushes(sems, 6)
    normed = normed_input(x(), gain())

    def put(g, at, piece):
        keys_s[g, :, at : at + 128] = piece

    def after(g):
        for yy in range(NY):
            push.start(keys_s.at[g], keys.at[yy * NG + g])

    pieces(dot(normed, w()), put, after)
    push.finish()


def k_queries_values(x, gain, wq, wv, qv0, qv1, qv2, qv3, x_s, g_s, wq_s, wv_s, qv, sems):
    x, gain, wq, wv = fetch((x, gain, wq, wv), (x_s, g_s, wq_s, wv_s), sems)
    normed = normed_input(x(), gain())
    for first, w in ((0, wq), (WIDTH, wv)):

        def put(g, at, piece, first=first):
            qv[g, :, first + at : first + at + 128] = piece

        pieces(dot(normed, w()), put)
    me = my_group()
    for k, out in enumerate((qv0, qv1, qv2, qv3)):
        out[...] = qv[me ^ k]


def rows_out(out, out_s, products, first, second, push):
    done = []
    for a in range(NS):
        while len(done) * I < (a + 1) * ROWS:
            done.append(products(len(done)))
        head = a * ROWS // I
        rows = jnp.concatenate(done[head:], axis=0)
        lo = a * ROWS - head * I
        t = slice(a * SENT, (a + 1) * SENT)
        rows = jnp.concatenate((rows[lo : lo + ROWS], first[t], second[t]), axis=0)
        out_s[a] = rows.astype(BF16)
        push.start(out_s.at[a], out.at[a])


def rows_in(parts):
    got = [parts[a].astype(F32) for a in range(NS)]
    first = jnp.concatenate([t[ROWS : ROWS + SENT] for t in got], axis=0)
    second = jnp.concatenate([t[ROWS + SENT :] for t in got], axis=0)
    return first, second


def k_logits(
    qv0, qv1, qv2, qv3, keys, x, cot, out, queries, values, out_s, q_s, v_s, sems
):
    push = Pushes(sems)
    me = my_group()
    for k, qv in enumerate((qv0, qv1, qv2, qv3)):
        q_s[me ^ k] = qv[:, 0:WIDTH]
        v_s[me ^ k] = qv[:, WIDTH : 2 * WIDTH]
    push.start(q_s, queries)
    push.start(v_s, values)
    perm = to_column()
    first = dot(perm, x[...].astype(F32).reshape(S * R, D).astype(BF16))
    second = dot(perm, cot[...].astype(F32).reshape(S * R, D).astype(BF16))

    def products(h):
        c = slice(h * 256, (h + 1) * 256)
        return dot_nt(q_s[:, :, c].reshape(I, 256), keys[:, c])

    rows_out(out, out_s, products, first, second, push)
    push.finish()


def summed(parts):
    total = parts[0].astype(F32)
    for a in range(1, NS):
        total = total + parts[a].astype(F32)
    return total[:ROWS]


def k_softmax(parts, values, probs, weights, p_s, sems):
    push = Pushes(sems)
    logits = summed(parts) * ROW_SCALE
    e = jnp.exp(logits - jnp.max(logits, axis=-1, keepdims=True))
    p = e * (1.0 / jnp.sum(e, axis=-1, keepdims=True))
    p_s[...] = p
    push.start(p_s, probs)
    w = p.astype(BF16)
    for a in range(NS):
        weights[a] = w
    push.finish()


def k_gather(v0, v1, v2, v3, out, values, sems):
    me = lax.axis_index("y")
    (own,) = fetch((v0,), (values.at[me],), sems, wait_only=True)
    push = Pushes(sems, 1)
    for k, v in enumerate((v1, v2, v3)):
        values[me ^ (k + 1)] = v[...]
    own()
    push.start(values, out)
    push.finish()


def k_attend(weights, values, out):
    perm = to_wide()
    for h in range(GH):
        c = slice(h * 256, (h + 1) * 256)
        v = values[:, :, c].reshape(NY * I, 256)
        att = dot(weights[h * I : (h + 1) * I], v).astype(BF16)
        out[:, c] = dot(perm, att).astype(BF16)


def k_column(
    att_in, sent, gain, out_row, wq, wk, wv, out_col, back, grad_out,
    wk_s, wv_s, oc_s, att_s, gq_s, gk_s, gv_s, sems,
):
    wk, wv, out_col = fetch((wk, wv, out_col), (wk_s, wv_s, oc_s), sems, cuts=2)
    raw = att_in[...].astype(F32).reshape(NS, NG, CP, WIDTH)
    groups = [raw[:, g].reshape(NS * CP, WIDTH) for g in range(NG)]
    per_seq = []
    for s in range(S):
        cols = []
        for fb in range(6):
            pair = []
            for n in (2 * fb, 2 * fb + 1):
                pair.append(blk(groups[n // GH], (n % GH) * 2 + s // 2))
            cols.append(halves(pair[0], pair[1], s % 2, s % 2))
        per_seq.append(jnp.concatenate(cols, axis=1).reshape(NS, 1, CP, D))
    att_row = jnp.concatenate(per_seq, axis=1).reshape(TOK, D).astype(BF16)
    pad = to_padded()
    att_row = dot_tn(pad, att_row).astype(BF16)
    xc, cot = rows_in(sent)
    cot = cot.astype(BF16)
    middle = (xc + dot(att_row, out_row[...])).astype(BF16)
    mid = middle.astype(F32)
    hat, r = moments(mid)
    normed = (hat * gain[...].reshape(1, D)).astype(BF16)
    q = dot(normed, wq[...]).astype(BF16) * jnp.asarray(COL_SCALE, BF16)
    k = dot(normed, wk()).astype(BF16)
    v = dot(normed, wv()).astype(BF16)
    ga = dot_nt(cot, out_col()).astype(BF16)
    row = lax.broadcasted_iota(jnp.int32, (2 * S * R, 1), 0)
    col = lax.broadcasted_iota(jnp.int32, (1, S * R), 1)
    same = (row % CR) == (col % CR)
    low = lax.broadcasted_iota(jnp.int32, (1, 128), 1) < 64
    masks = [jnp.where(low == first, 1.0, 0.0).astype(BF16) for first in (True, False)]

    def stack(t):
        return jnp.concatenate([t * masks[0], t * masks[1]], axis=0)

    def unstack(t):
        return jnp.where(low, t[: S * R], t[S * R :])

    for fb in range(6):
        at = slice(fb * 128, (fb + 1) * 128)
        kb, vb = blk(k, fb), blk(v, fb)
        qs, gs = stack(blk(q, fb)), stack(blk(ga, fb))
        logits = jnp.where(same, dot_nt(qs, kb), -1e30)
        e = jnp.exp(logits - jnp.max(logits, axis=-1, keepdims=True))
        p = e * (1.0 / jnp.sum(e, axis=-1, keepdims=True))
        w = p.astype(BF16)
        grads = dot_nt(gs, vb)
        dl = (p * (grads - jnp.sum(p * grads, axis=-1, keepdims=True))).astype(BF16)
        att_s[:, at] = unstack(dot(w, vb)).astype(BF16)
        gq_s[:, at] = (unstack(dot(dl, kb)) * COL_SCALE).astype(BF16)
        gk_s[:, at] = dot_tn(dl, qs).astype(BF16)
        gv_s[:, at] = dot_tn(w, gs).astype(BF16)
    back[:, 0:D] = (mid + dot(att_s[...], out_col())).astype(BF16)
    gn = (
        dot_nt(gq_s[...], wq[...]) + dot_nt(gk_s[...], wk()) + dot_nt(gv_s[...], wv())
    )
    gmid = (cot.astype(F32) + norm_grad(gn, gain[...].reshape(1, D), hat, r)).astype(BF16)
    back[:, D : 2 * D] = gmid
    gra = dot_nt(gmid, out_row[...]).astype(BF16)
    gra = dot(pad, gra).reshape(NS, S, CP, D)
    seqs = [gra[:, s].reshape(NS * CP, D) for s in range(S)]
    per_group = []
    for g in range(NG):
        cols = []
        for h in range(GH):
            n = g * GH + h
            for sp in range(2):
                cols.append(
                    halves(blk(seqs[2 * sp], n // 2), blk(seqs[2 * sp + 1], n // 2), n % 2, n % 2)
                )
        per_group.append(jnp.concatenate(cols, axis=1).reshape(NS, 1, CP, WIDTH))
    grad_out[...] = jnp.concatenate(per_group, axis=1).reshape(TOK, WIDTH).astype(BF16)


def k_grad_probs(grads, values, back, gra, out, gra_s, out_s, sems):
    push = Pushes(sems)
    perm = to_wide()
    for h in range(GH):
        c = slice(h * 256, (h + 1) * 256)
        gra_s[:, c] = dot_tn(perm, grads[:, c]).astype(BF16)
    push.start(gra_s, gra)
    first, second = back[:, 0:D].astype(F32), back[:, D : 2 * D].astype(F32)

    def products(h):
        c = slice(h * 256, (h + 1) * 256)
        return dot_nt(gra_s[:, c], values[:, :, c].reshape(NY * I, 256))

    rows_out(out, out_s, products, first, second, push)
    push.finish()


def k_grad_values(weights, gra, gv0, gv1, gv2, gv3, gv, sems):
    for h in range(GH):
        c = slice(h * 256, (h + 1) * 256)
        t = dot_tn(weights[h * I : (h + 1) * I], gra[:, c]).astype(BF16)
        gv[:, :, c] = t.reshape(NY, I, 256)
    me = lax.axis_index("y")
    push = Pushes(sems)
    push.start(gv.at[me], gv0)
    for k, out in enumerate((gv1, gv2, gv3)):
        out[...] = gv[me ^ (k + 1)]
    push.finish()


def k_sum_values(gv0, gv1, gv3, gv, g_s, gv_s, sems):
    (gv0,) = fetch((gv0,), (g_s,), sems)
    push = Pushes(sems, 1)
    total = gv1[...].astype(F32) + gv3[...].astype(F32)
    gv_s[...] = total + gv0().astype(F32)
    push.start(gv_s, gv)
    push.finish()


def k_softmax_grad(parts, probs, gv, out, p_s, out_s, sems):
    (probs,) = fetch((probs,), (p_s,), sems)
    push = Pushes(sems, 1)
    grads = summed(parts)
    p = probs()
    dl = p * (grads - jnp.sum(p * grads, axis=-1, keepdims=True)) * ROW_SCALE
    out_s[...] = dl.astype(BF16)
    for a in range(NS):
        push.start(out_s, out.at[a])
    push.finish()


def k_grad_keys(dl, queries, before, gk, q_s, gk_s, sems):
    (queries,) = fetch((queries,), (q_s,), sems)
    push = Pushes(sems, 1)
    queries = queries()
    for h in range(GH):
        c = slice(h * 256, (h + 1) * 256)
        gk_s[:, c] = dot_tn(dl[h * I : (h + 1) * I], queries[:, c]).astype(BF16)
        for r in (slice(0, D // 2), slice(D // 2, D)):
            push.start(gk_s.at[r, c], gk.at[r, c])
    push.finish()


def k_grad_queries(
    dl, keys, gv, gv2, gqv0, gqv1, gqv2, gqv3,
    sum_s, two_s, gv_s, gq_s, o0, o1, o2, o3, sems,
):
    gv, gv2 = fetch((gv, gv2), (sum_s, two_s), sems)
    push = Pushes(sems, 2)
    for h in range(GH):
        c = slice(h * 256, (h + 1) * 256)
        gq_s[:, :, c] = dot(dl[h * I : (h + 1) * I], keys[:, c]).astype(BF16).reshape(NG, R, 256)
    gv_s[...] = (gv() + gv2().astype(F32)).astype(BF16).reshape(NG, R, WIDTH)
    me = my_group()
    for k, (held, out) in enumerate(zip((o0, o1, o2, o3), (gqv0, gqv1, gqv2, gqv3))):
        held[:, 0:WIDTH] = gq_s[me ^ k]
        held[:, WIDTH : 2 * WIDTH] = gv_s[me ^ k]
        push.start(held, out)
    push.finish()


def k_block_out(sent, out):
    first, _ = rows_in(sent)
    out[...] = dot_tn(to_column(), first.astype(BF16)).reshape(S, R, D).astype(BF16)


def token_rows(groups):
    rows = []
    for s in range(S):
        cols = []
        for fb in range(6):
            pair = []
            for n in (2 * fb, 2 * fb + 1):
                pair.append(blk(groups[n // GH], (n % GH) * 2 + s // 2))
            cols.append(halves(pair[0], pair[1], s % 2, s % 2))
        rows.append(jnp.concatenate(cols, axis=1))
    return jnp.concatenate(rows, axis=0).astype(BF16)


def k_finish_keys(gk, wk, out, gk_s, wk_s, out_s, sems):
    gk, wk = fetch((gk, wk), (gk_s, wk_s), sems, cuts=3)
    push = Pushes(sems, 6)
    gk()
    groups = []
    for g in range(NG):
        t = gk_s[g * R : (g + 1) * R].astype(F32)
        for yy in range(1, NY):
            lo = (yy * NG + g) * R
            t = t + gk_s[lo : lo + R].astype(F32)
        groups.append(t)
    out_s[...] = dot_nt(token_rows(groups), wk())
    push.start(out_s, out)
    push.finish()


def k_finish(
    gqv0, gqv1, gqv2, gqv3, part, x, sent, gain, wq, wv, input_grad,
    gqv, own_s, part_s, sems,
):
    gqv0, part = fetch((gqv0, part), (own_s, part_s), sems)
    me = my_group()
    for k, got in enumerate((gqv1, gqv2, gqv3)):
        gqv[me ^ (k + 1)] = got[...]
    perm = to_column()
    _, second = rows_in(sent)
    gmid = dot_tn(perm, second.astype(BF16))
    hat, r = moments(x[...].astype(F32).reshape(S * R, D))
    gqv[me] = gqv0()
    total = None
    for first, w in ((0, wq), (WIDTH, wv)):
        groups = [gqv[g, :, first : first + WIDTH].astype(F32) for g in range(NG)]
        t = dot_nt(token_rows(groups), w[...])
        total = t if total is None else total + t
    total = total + part()
    grad = gmid + norm_grad(total, gain[...].reshape(1, D), hat, r)
    input_grad[...] = grad.reshape(S, R, D).astype(BF16)


def swap(x, axes):
    return lax.all_to_all(x, axes, split_axis=0, concat_axis=0, tiled=True)


def spread(parts, axes):
    n = len(parts)
    pairs = [[(i, i ^ k) for i in range(n)] for k in range(n)]
    return [parts[0]] + [lax.ppermute(parts[k], axes, pairs[k]) for k in range(1, n)]


def local(
    x,
    cot,
    gain_row,
    query_row,
    key_row,
    value_row,
    out_row,
    gain_col,
    query_col,
    key_col,
    value_col,
    out_col,
):
    piece = ((R, 2 * WIDTH), BF16)
    block = ((NS, BLOCK, NY * I), BF16)
    part = ((NG, R, WIDTH), BF16)
    weight = pltpu.VMEM((D, D), BF16)
    row = pltpu.VMEM((S, R, D), BF16)
    gain = pltpu.VMEM((D,), F32)
    keys = call(
        k_keys,
        [pltpu.HBM((NY * NG, R, WIDTH), BF16)],
        x, gain_row, key_row,
        far=(0, 1, 2),
        sems=6 + NY * NG,
        scratch=[row, gain, weight, pltpu.VMEM(*part)],
    )
    qv = call(
        k_queries_values,
        [piece] * NG,
        x, gain_row, query_row, value_row,
        far=(0, 1, 2, 3),
        sems=4,
        scratch=[row, gain, weight, weight, pltpu.VMEM((NG, R, 2 * WIDTH), BF16)],
    )
    qv = spread(qv, GRP)
    keys = swap(keys, ALLRES).reshape(NY * I, WIDTH)
    parts, queries, values = call(
        k_logits,
        [pltpu.HBM(*block), pltpu.HBM(*part), pltpu.HBM(*part)],
        *qv, keys, x, cot,
        sems=2 + NS,
        scratch=[pltpu.VMEM(*block), pltpu.VMEM(*part), pltpu.VMEM(*part)],
    )
    queries = queries.reshape(I, WIDTH)
    parts = swap(parts, SEQ)
    values = spread([values.reshape(I, WIDTH)] * NY, "y")
    gathered = pltpu.VMEM((NY, I, WIDTH), BF16)
    values = call(
        k_gather,
        [pltpu.HBM((NY, I, WIDTH), BF16)],
        *values,
        far=(0,),
        sems=2,
        scratch=[gathered],
    )
    probs, weights = call(
        k_softmax,
        [pltpu.HBM((ROWS, NY * I), F32), ((NS, ROWS, NY * I), BF16)],
        parts, values,
        far=(1,),
        sems=1,
        scratch=[pltpu.VMEM((ROWS, NY * I), F32)],
    )
    weights = swap(weights, SEQ).reshape(GH * I, NY * I)
    att = call(k_attend, [((TOK, WIDTH), BF16)], weights, values)
    att = swap(att, WIDE)
    back, grads = call(
        k_column,
        [((S * R, 2 * D), BF16), ((TOK, WIDTH), BF16)],
        att, parts, gain_col, out_row, query_col, key_col, value_col, out_col,
        mem=32,
        far=(5, 6, 7),
        sems=6,
        scratch=[weight] * 3 + [pltpu.VMEM((S * R, D), BF16)] * 4,
    )
    grads = swap(grads, WIDE)
    gra, gparts = call(
        k_grad_probs,
        [pltpu.HBM((I, WIDTH), BF16), pltpu.HBM(*block)],
        grads, values, back,
        sems=1 + NS,
        scratch=[pltpu.VMEM((I, WIDTH), BF16), pltpu.VMEM(*block)],
    )
    gparts = swap(gparts, SEQ)
    gv = call(
        k_grad_values,
        [pltpu.HBM((I, WIDTH), BF16)] + [((I, WIDTH), BF16)] * (NY - 1),
        weights, gra,
        sems=1,
        scratch=[gathered],
    )
    gv = spread(gv, "y")
    summand = pltpu.VMEM((I, WIDTH), BF16)
    sum_s = pltpu.VMEM((I, WIDTH), F32)
    some = call(
        k_sum_values,
        [pltpu.HBM((I, WIDTH), F32)],
        gv[0], gv[1], gv[3],
        far=(0,),
        sems=2,
        scratch=[summand, sum_s],
    )
    dl = call(
        k_softmax_grad,
        [pltpu.HBM((NS, ROWS, NY * I), BF16)],
        gparts, probs, some,
        far=(1, 2),
        sems=1 + NS,
        scratch=[pltpu.VMEM((ROWS, NY * I), F32), pltpu.VMEM((ROWS, NY * I), BF16)],
    )
    dl = swap(dl, SEQ).reshape(GH * I, NY * I)
    gk = call(
        k_grad_keys,
        [pltpu.HBM((D, D), BF16)],
        dl, queries, gv[2],
        far=(1, 2),
        sems=2 * GH + 1,
        scratch=[summand, weight],
    )
    gqv = call(
        k_grad_queries,
        [pltpu.HBM(*piece)] * NG,
        dl, keys, some, gv[2],
        far=(2, 3),
        sems=2 + NG,
        scratch=[sum_s, summand, pltpu.VMEM(*part), pltpu.VMEM(*part)] + [pltpu.VMEM(*piece)] * NG,
    )
    gqv = spread(gqv, GRP)
    gk = swap(gk, ALLRES).reshape(NY * I, WIDTH)
    block_out = call(k_block_out, [((S, R, D), BF16)], gparts)
    total = pltpu.VMEM((S * R, D), F32)
    from_keys = call(
        k_finish_keys,
        [pltpu.HBM((S * R, D), F32)],
        gk, key_row,
        cost=pl.CostEstimate(flops=4 * 10**9, bytes_accessed=3 * 10**6, transcendentals=0),
        far=(0, 1),
        sems=7,
        scratch=[weight, weight, total],
    )
    input_grad = call(
        k_finish,
        [((S, R, D), BF16)],
        *gqv, from_keys, x, gparts, gain_row, query_row, value_row,
        far=(0, 4),
        sems=2,
        scratch=[
            pltpu.VMEM((NG, R, 2 * WIDTH), BF16),
            pltpu.VMEM(*piece),
            total,
        ],
    )
    return block_out, input_grad


def solution(mesh):
    fine = Mesh(mesh.devices.reshape(2, 4, 2, 4, 2), ("xh", "z", "xl", "y", "c"))
    spec = P(("xh", "z"), ("xl", "y", "c"), None)
    return jax.shard_map(
        local,
        mesh=fine,
        in_specs=(spec, spec) + (P(),) * 10,
        out_specs=(spec, spec),
        check_vma=False,
    )
```

profile of v0, /device:TPU:1, one launch (start us, length us, event | category | flops | bytes accessed | tf_op | source)
XLA Modules:
  0.0 199.4 jit_solution(7637418864967703055)
XLA Ops:
  0.6 2.9 %shard_map.132 = bf16[16,48,768]{2,1,0:T(8,128)(2,1)} custom-call(bf16[4,48,768]{2,1,0:T(8,128)(2,1)} %x.7, f32[768]{0:T(1024)} %gain.7, bf16[768,768]{1,0:T(8,128)(2,1)} %wk.3), custom_call_target="tpu_custom_call" | custom-call | tf_op jit(solution)/shard_map/pallas_call | solution.py:58
  3.6 6.9 %all-to-all-start = ((bf16[16,48,768]{2,1,0:T(8,128)(2,1)}), bf16[16,48,768]{2,1,0:T(8,128)(2,1)S(1)}, u32[]{:S(2)}, u32[]{:S(2)}) async-start(bf16[16,48,768]{2,1,0:T(8,128)(2,1)} %shard_map.132), calls=%async_computation | async-start | bytes 2359296 | tf_op jit(solution)/shard_map/all_to_all | solution.py:508
  10.5 2.6 %shard_map.131 = (bf16[48,1536]{1,0:T(8,128)(2,1)S(1)}, bf16[48,1536]{1,0:T(8,128)(2,1)S(1)}, bf16[48,1536]{1,0:T(8,128)(2,1)S(1)}, bf16[48,1536]{1,0:T(8,128)(2,1)S(1)}) custom-call(bf16[4,48,768]{2,1,0:T(8,128)(2,1)} %x.7, f32[768]{0:T(1024)} %gain.7, bf16[768,768]{1,0:T(8,128)(2,1)} %wq.5, bf16[768,768]{1,0:T(8,128)(2,1)} %wv.5), custom_call_target="tpu_custom_call" | custom-call | tf_op jit(solution)/shard_map/pallas_call | solution.py:58
  15.4 13.7 %collective-permute-done.1.qv2 = bf16[48,1536]{1,0:T(8,128)(2,1)S(1)} collective-permute-done((bf16[48,1536]{1,0:T(8,128)(2,1)S(1)}, bf16[48,1536]{1,0:T(8,128)(2,1)S(1)}, u32[]{:S(2)}, u32[]{:S(2)}) %collective-permute-start.1) | collective-permute-done | bytes 147488 | tf_op jit(solution)/shard_map/ppermute | solution.py:514
  29.0 3.3 %collective-permute-done.2.qv3 = bf16[48,1536]{1,0:T(8,128)(2,1)S(1)} collective-permute-done((bf16[48,1536]{1,0:T(8,128)(2,1)S(1)}, bf16[48,1536]{1,0:T(8,128)(2,1)S(1)}, u32[]{:S(2)}, u32[]{:S(2)}) %collective-permute-start.2) | collective-permute-done | bytes 147488 | tf_op jit(solution)/shard_map/ppermute | solution.py:514
  32.4 1.7 shard_map.133
  34.1 7.3 %all-to-all-start.1 = ((bf16[8,120,768]{2,1,0:T(8,128)(2,1)}), bf16[8,120,768]{2,1,0:T(8,128)(2,1)S(1)}, u32[]{:S(2)}, u32[]{:S(2)}) async-start(bf16[8,120,768]{2,1,0:T(8,128)(2,1)} %get-tuple-element.27), calls=%async_computation.1 | async-start | bytes 2949120 | tf_op jit(solution)/shard_map/all_to_all | solution.py:508
  41.4 2.3 %collective-permute-start.5 = (bf16[192,768]{1,0:T(8,128)(2,1)S(1)}, bf16[192,768]{1,0:T(8,128)(2,1)S(1)}, u32[]{:S(2)}, u32[]{:S(2)}) collective-permute-start(bf16[192,768]{1,0:T(8,128)(2,1)S(1)} %bitcast.23), channel_id=1, source_target_pairs={{0,6},{2,4},{4,2},{6,0},{1,7},{3,5},{5,3},{7,1},{8,14},{10,12},{12... | collective-permute-start | bytes 884744 | tf_op jit(solution)/shard_map/ppermute | solution.py:514
  44.8 12.4 %collective-permute-done.5.v3 = bf16[192,768]{1,0:T(8,128)(2,1)S(1)} collective-permute-done((bf16[192,768]{1,0:T(8,128)(2,1)S(1)}, bf16[192,768]{1,0:T(8,128)(2,1)S(1)}, u32[]{:S(2)}, u32[]{:S(2)}) %collective-permute-start.5) | collective-permute-done | bytes 294944 | tf_op jit(solution)/shard_map/ppermute | solution.py:514
  57.5 2.0 %shard_map.134.values = bf16[4,192,768]{2,1,0:T(8,128)(2,1)} custom-call(bf16[192,768]{1,0:T(8,128)(2,1)} %bitcast.22, bf16[192,768]{1,0:T(8,128)(2,1)S(1)} %collective-permute-done.3.v1, bf16[192,768]{1,0:T(8,128)(2,1)S(1)} %collective-permute-done.4.v2, bf16[192,768]{1,0:T(8,128)(2,1)S(1)} %collective-permute-done.5.v3), custom_call_target="tpu_custom_call" | custom-call | tf_op jit(solution)/shard_map/pallas_call | solution.py:58
  62.0 18.5 %all_to_all.58 = bf16[8,72,768]{2,1,0:T(8,128)(2,1)S(1)} all-to-all(bf16[8,72,768]{2,1,0:T(8,128)(2,1)S(1)} %get-tuple-element.29), channel_id=1, replica_groups=mesh['xh'=2,'z'=4,'xl'=2,'y'=4,'c'=2] {'xh','z'}, dimensions={0} | all-to-all | bytes 1769472 | tf_op jit(solution)/shard_map/all_to_all | solution.py:508
  81.5 15.6 %all_to_all.59 = bf16[32,8,768]{2,1,0:T(8,128)(2,1)S(1)} all-to-all(bf16[32,8,768]{2,1,0:T(8,128)(2,1)S(1)} %bitcast.18), channel_id=1, replica_groups=mesh['xh'=2,'z'=4,'xl'=2,'y'=4,'c'=2] {'xh','z','xl','c'}, dimensions={0} | all-to-all | bytes 786432 | tf_op jit(solution)/shard_map/all_to_all | solution.py:508
  97.2 9.3 %shard_map.137 = (bf16[192,1536]{1,0:T(8,128)(2,1)S(1)}, bf16[256,768]{1,0:T(8,128)(2,1)S(1)}) custom-call(bf16[256,768]{1,0:T(8,128)(2,1)S(1)} %bitcast.17, bf16[8,120,768]{2,1,0:T(8,128)(2,1)S(1)} %all-to-all-done.1.parts.sent, f32[768]{0:T(1024)S(1)} %copy-done.10, bf16[768,768]{1,0:T(8,128)(2,1)S(1)} %copy-done.5, bf16[768,768]{1,0:T(8,128)(2,1)S(1)} %copy-done.6, ...), custom_call_target="tpu_custom_call" | custom-call | tf_op jit(solution)/shard_map/pallas_call | solution.py:58
  106.5 14.1 %all_to_all.60 = bf16[32,8,768]{2,1,0:T(8,128)(2,1)S(1)} all-to-all(bf16[32,8,768]{2,1,0:T(8,128)(2,1)S(1)} %bitcast.20), channel_id=1, replica_groups=mesh['xh'=2,'z'=4,'xl'=2,'y'=4,'c'=2] {'xh','z','xl','c'}, dimensions={0} | all-to-all | bytes 786432 | tf_op jit(solution)/shard_map/all_to_all | solution.py:508
  120.6 1.7 shard_map.138
  122.2 3.6 %all-to-all-start.5 = ((bf16[8,120,768]{2,1,0:T(8,128)(2,1)}), bf16[8,120,768]{2,1,0:T(8,128)(2,1)S(1)}, u32[]{:S(2)}, u32[]{:S(2)}) async-start(bf16[8,120,768]{2,1,0:T(8,128)(2,1)} %get-tuple-element.32), calls=%async_computation.5 | async-start | bytes 2949120 | tf_op jit(solution)/shard_map/all_to_all | solution.py:508
  129.7 1.9 collective-permute-start.7
  131.6 4.7 %collective-permute-done.6.gv1 = bf16[192,768]{1,0:T(8,128)(2,1)S(1)} collective-permute-done((bf16[192,768]{1,0:T(8,128)(2,1)S(1)}, bf16[192,768]{1,0:T(8,128)(2,1)S(1)}, u32[]{:S(2)}, u32[]{:S(2)}) %collective-permute-start.6) | collective-permute-done | bytes 294944 | tf_op jit(solution)/shard_map/ppermute | solution.py:514
  136.2 1.9 collective-permute-done.7.gv3
  138.1 1.8 shard_map.141.gv
  140.0 4.7 %all-to-all-done.5.sent.parts = bf16[8,120,768]{2,1,0:T(8,128)(2,1)S(1)} async-done(((bf16[8,120,768]{2,1,0:T(8,128)(2,1)}), bf16[8,120,768]{2,1,0:T(8,128)(2,1)S(1)}, u32[]{:S(2)}, u32[]{:S(2)}) %all-to-all-start.5) | async-done | bytes 1474592 | tf_op jit(solution)/shard_map/all_to_all | solution.py:508
  144.7 2.1 %shard_map.142 = bf16[8,72,768]{2,1,0:T(8,128)(2,1)} custom-call(bf16[8,120,768]{2,1,0:T(8,128)(2,1)S(1)} %all-to-all-done.5.sent.parts, f32[72,768]{1,0:T(8,128)} %get-tuple-element.33.probs, f32[192,768]{1,0:T(8,128)} %shard_map.141.gv), custom_call_target="tpu_custom_call" | custom-call | tf_op jit(solution)/shard_map/pallas_call | solution.py:58
  146.7 5.8 %all-to-all-start.6 = ((bf16[8,72,768]{2,1,0:T(8,128)(2,1)}), bf16[8,72,768]{2,1,0:T(8,128)(2,1)S(1)}, u32[]{:S(2)}, u32[]{:S(2)}) async-start(bf16[8,72,768]{2,1,0:T(8,128)(2,1)} %shard_map.142), calls=%async_computation.6 | async-start | bytes 1769472 | tf_op jit(solution)/shard_map/all_to_all | solution.py:508
  152.5 2.5 %collective-permute-start.8 = (bf16[192,768]{1,0:T(8,128)(2,1)}, bf16[192,768]{1,0:T(8,128)(2,1)}, u32[]{:S(2)}, u32[]{:S(2)}) collective-permute-start(bf16[192,768]{1,0:T(8,128)(2,1)} %copy-done.11), channel_id=1, source_target_pairs={{0,4},{2,6},{4,0},{6,2},{1,5},{3,7},{5,1},{7,3},{8,12},{10,14},{12... | collective-permute-start | bytes 884744 | tf_op jit(solution)/shard_map/ppermute | solution.py:514
  155.0 7.1 %collective-permute-done.8.gv2.before = bf16[192,768]{1,0:T(8,128)(2,1)} collective-permute-done((bf16[192,768]{1,0:T(8,128)(2,1)}, bf16[192,768]{1,0:T(8,128)(2,1)}, u32[]{:S(2)}, u32[]{:S(2)}) %collective-permute-start.8) | collective-permute-done | bytes 294944 | tf_op jit(solution)/shard_map/ppermute | solution.py:514
  162.1 3.0 %all-to-all-done.6 = bf16[8,72,768]{2,1,0:T(8,128)(2,1)S(1)} async-done(((bf16[8,72,768]{2,1,0:T(8,128)(2,1)}), bf16[8,72,768]{2,1,0:T(8,128)(2,1)S(1)}, u32[]{:S(2)}, u32[]{:S(2)}) %all-to-all-start.6) | async-done | bytes 884768 | tf_op jit(solution)/shard_map/all_to_all | solution.py:508
  165.1 2.5 %shard_map.144 = bf16[768,768]{1,0:T(8,128)(2,1)} custom-call(bf16[576,768]{1,0:T(8,128)(2,1)S(1)} %bitcast.15, bf16[192,768]{1,0:T(8,128)(2,1)} %bitcast.26, bf16[192,768]{1,0:T(8,128)(2,1)} %collective-permute-done.8.gv2.before), custom_call_target="tpu_custom_call" | custom-call | tf_op jit(solution)/shard_map/pallas_call | solution.py:58
  167.6 6.8 %all-to-all-start.7 = ((bf16[16,48,768]{2,1,0:T(8,128)(2,1)}), bf16[16,48,768]{2,1,0:T(8,128)(2,1)}, u32[]{:S(2)}, u32[]{:S(2)}) async-start(bf16[16,48,768]{2,1,0:T(8,128)(2,1)} %bitcast.21), calls=%async_computation.7 | async-start | bytes 2359296 | tf_op jit(solution)/shard_map/all_to_all | solution.py:508
  175.4 2.4 %shard_map.143 = (bf16[48,1536]{1,0:T(8,128)(2,1)}, bf16[48,1536]{1,0:T(8,128)(2,1)}, bf16[48,1536]{1,0:T(8,128)(2,1)}, bf16[48,1536]{1,0:T(8,128)(2,1)}) custom-call(bf16[576,768]{1,0:T(8,128)(2,1)S(1)} %bitcast.16, bf16[768,768]{1,0:T(8,128)(2,1)S(1)} %bitcast.12, f32[192,768]{1,0:T(8,128)} %shard_map.141.gv, ...), custom_call_target="tpu_custom_call" | custom-call | tf_op jit(solution)/shard_map/pallas_call | solution.py:58
  180.2 11.6 %all-to-all-done.7 = bf16[16,48,768]{2,1,0:T(8,128)(2,1)} async-done(((bf16[16,48,768]{2,1,0:T(8,128)(2,1)}), bf16[16,48,768]{2,1,0:T(8,128)(2,1)}, u32[]{:S(2)}, u32[]{:S(2)}) %all-to-all-start.7) | async-done | bytes 1179680 | tf_op jit(solution)/shard_map/all_to_all | solution.py:508
  191.9 3.2 %shard_map.145.part = f32[192,768]{1,0:T(8,128)} custom-call(bf16[768,768]{1,0:T(8,128)(2,1)} %bitcast.10.gk, bf16[768,768]{1,0:T(8,128)(2,1)} %wk.3), custom_call_target="tpu_custom_call" | custom-call | flops 4000000000 | bytes 3000000 | tf_op jit(solution)/shard_map/pallas_call | solution.py:58
  196.3 2.9 %shard_map.146 = bf16[4,48,768]{2,1,0:T(8,128)(2,1)} custom-call(bf16[48,1536]{1,0:T(8,128)(2,1)} %get-tuple-element.39.gqv0, bf16[48,1536]{1,0:T(8,128)(2,1)S(1)} %collective-permute-done.9.gqv1, bf16[48,1536]{1,0:T(8,128)(2,1)S(1)} %collective-permute-done.10.gqv2, bf16[48,1536]{1,0:T(8,128)(2,1)S(1)} %collective-permute-done.11.gqv3, ...), custom_call_target="tpu_custom_call" | custom-call | tf_op jit(solution)/shard_map/pallas_call | solution.py:58
  (47 shorter events, 15.7 us)
Async XLA Ops:
  3.6 28.8 %all-to-all-start = ((bf16[16,48,768]{2,1,0:T(8,128)(2,1)}), bf16[16,48,768]{2,1,0:T(8,128)(2,1)S(1)}, u32[]{:S(2)}, u32[]{:S(2)}) async-start(bf16[16,48,768]{2,1,0:T(8,128)(2,1)} %shard_map.132), calls=%async_computation | async-start | bytes 2359296 | tf_op jit(solution)/shard_map/all_to_all | solution.py:508
  10.5 21.9 %copy-start.1 = (bf16[4,48,768]{2,1,0:T(8,128)(2,1)S(1)}, bf16[4,48,768]{2,1,0:T(8,128)(2,1)}, u32[]{:S(2)}) copy-start(bf16[4,48,768]{2,1,0:T(8,128)(2,1)} %x.7) | copy-start | bytes 884740
  10.5 21.9 %copy-start.7 = (bf16[4,48,768]{2,1,0:T(8,128)(2,1)S(1)}, bf16[4,48,768]{2,1,0:T(8,128)(2,1)}, u32[]{:S(2)}) copy-start(bf16[4,48,768]{2,1,0:T(8,128)(2,1)} %cot.1) | copy-start | bytes 884740
  13.1 2.2 %collective-permute-start = (bf16[48,1536]{1,0:T(8,128)(2,1)S(1)}, bf16[48,1536]{1,0:T(8,128)(2,1)S(1)}, u32[]{:S(2)}, u32[]{:S(2)}) collective-permute-start(bf16[48,1536]{1,0:T(8,128)(2,1)S(1)} %get-tuple-element.24), channel_id=1, source_target_pairs={{0,1},{1,0},{8,9},{9,8},{2,3},{3,2},{10,11},{11,10},{4,5},{5,4},{1... | collective-permute-start | bytes 442376 | tf_op jit(solution)/shard_map/ppermute | solution.py:514
  13.3 15.7 %collective-permute-start.1 = (bf16[48,1536]{1,0:T(8,128)(2,1)S(1)}, bf16[48,1536]{1,0:T(8,128)(2,1)S(1)}, u32[]{:S(2)}, u32[]{:S(2)}) collective-permute-start(bf16[48,1536]{1,0:T(8,128)(2,1)S(1)} %get-tuple-element.25), channel_id=1, source_target_pairs={{0,8},{1,9},{8,0},{9,1},{2,10},{3,11},{10,2},{11,3},{4,12},{5,13},... | collective-permute-start | bytes 442376 | tf_op jit(solution)/shard_map/ppermute | solution.py:514
  15.0 17.4 %collective-permute-start.2 = (bf16[48,1536]{1,0:T(8,128)(2,1)S(1)}, bf16[48,1536]{1,0:T(8,128)(2,1)S(1)}, u32[]{:S(2)}, u32[]{:S(2)}) collective-permute-start(bf16[48,1536]{1,0:T(8,128)(2,1)S(1)} %get-tuple-element.26), channel_id=1, source_target_pairs={{0,9},{1,8},{8,1},{9,0},{2,11},{3,10},{10,3},{11,2},{4,13},{5,12},... | collective-permute-start | bytes 442376 | tf_op jit(solution)/shard_map/ppermute | solution.py:514
  34.1 7.4 %copy-start.12 = (bf16[4,48,768]{2,1,0:T(8,128)(2,1)S(1)}, bf16[4,48,768]{2,1,0:T(8,128)(2,1)}, u32[]{:S(2)}) copy-start(bf16[4,48,768]{2,1,0:T(8,128)(2,1)} %get-tuple-element.28) | copy-start | bytes 884740
  34.1 26.9 %all-to-all-start.1 = ((bf16[8,120,768]{2,1,0:T(8,128)(2,1)}), bf16[8,120,768]{2,1,0:T(8,128)(2,1)S(1)}, u32[]{:S(2)}, u32[]{:S(2)}) async-start(bf16[8,120,768]{2,1,0:T(8,128)(2,1)} %get-tuple-element.27), calls=%async_computation.1 | async-start | bytes 2949120 | tf_op jit(solution)/shard_map/all_to_all | solution.py:508
  41.4 15.7 %collective-permute-start.5 = (bf16[192,768]{1,0:T(8,128)(2,1)S(1)}, bf16[192,768]{1,0:T(8,128)(2,1)S(1)}, u32[]{:S(2)}, u32[]{:S(2)}) collective-permute-start(bf16[192,768]{1,0:T(8,128)(2,1)S(1)} %bitcast.23), channel_id=1, source_target_pairs={{0,6},{2,4},{4,2},{6,0},{1,7},{3,5},{5,3},{7,1},{8,14},{10,12},{12... | collective-permute-start | bytes 884744 | tf_op jit(solution)/shard_map/ppermute | solution.py:514
  43.7 13.4 %collective-permute-start.4 = (bf16[192,768]{1,0:T(8,128)(2,1)S(1)}, bf16[192,768]{1,0:T(8,128)(2,1)S(1)}, u32[]{:S(2)}, u32[]{:S(2)}) collective-permute-start(bf16[192,768]{1,0:T(8,128)(2,1)S(1)} %bitcast.24), channel_id=1, source_target_pairs={{0,4},{2,6},{4,0},{6,2},{1,5},{3,7},{5,1},{7,3},{8,12},{10,14},{12... | collective-permute-start | bytes 884744 | tf_op jit(solution)/shard_map/ppermute | solution.py:514
  44.2 13.2 %collective-permute-start.3 = (bf16[192,768]{1,0:T(8,128)(2,1)S(1)}, bf16[192,768]{1,0:T(8,128)(2,1)S(1)}, u32[]{:S(2)}, u32[]{:S(2)}) collective-permute-start(bf16[192,768]{1,0:T(8,128)(2,1)S(1)} %bitcast.25), channel_id=1, source_target_pairs={{0,2},{2,0},{4,6},{6,4},{1,3},{3,1},{5,7},{7,5},{8,10},{10,8},{12,... | collective-permute-start | bytes 884744 | tf_op jit(solution)/shard_map/ppermute | solution.py:514
  62.0 18.5 %copy-start = (bf16[4,192,768]{2,1,0:T(8,128)(2,1)S(1)}, bf16[4,192,768]{2,1,0:T(8,128)(2,1)}, u32[]{:S(2)}) copy-start(bf16[4,192,768]{2,1,0:T(8,128)(2,1)} %shard_map.134.values) | copy-start | bytes 3538948
  80.4 16.7 %copy-start.5 = (bf16[768,768]{1,0:T(8,128)(2,1)S(1)}, bf16[768,768]{1,0:T(8,128)(2,1)}, u32[]{:S(2)}) copy-start(bf16[768,768]{1,0:T(8,128)(2,1)} %out_row.1) | copy-start | bytes 3538948
  80.4 16.7 %copy-start.6 = (bf16[768,768]{1,0:T(8,128)(2,1)S(1)}, bf16[768,768]{1,0:T(8,128)(2,1)}, u32[]{:S(2)}) copy-start(bf16[768,768]{1,0:T(8,128)(2,1)} %wq.4) | copy-start | bytes 3538948
  80.4 16.7 %copy-start.10 = (f32[768]{0:T(1024)S(1)}, f32[768]{0:T(1024)}, u32[]{:S(2)}) copy-start(f32[768]{0:T(1024)} %gain.6) | copy-start | bytes 9220
  122.2 22.4 %all-to-all-start.5 = ((bf16[8,120,768]{2,1,0:T(8,128)(2,1)}), bf16[8,120,768]{2,1,0:T(8,128)(2,1)S(1)}, u32[]{:S(2)}, u32[]{:S(2)}) async-start(bf16[8,120,768]{2,1,0:T(8,128)(2,1)} %get-tuple-element.32), calls=%async_computation.5 | async-start | bytes 2949120 | tf_op jit(solution)/shard_map/all_to_all | solution.py:508
  125.8 1.0 copy-start.8
  128.1 0.7 copy-start.11
  128.8 7.5 %collective-permute-start.6 = (bf16[192,768]{1,0:T(8,128)(2,1)S(1)}, bf16[192,768]{1,0:T(8,128)(2,1)S(1)}, u32[]{:S(2)}, u32[]{:S(2)}) collective-permute-start(bf16[192,768]{1,0:T(8,128)(2,1)S(1)} %get-tuple-element.36), channel_id=1, source_target_pairs={{0,2},{2,0},{4,6},{6,4},{1,3},{3,1},{5,7},{7,5},{8,10},{10,8},{12,... | collective-permute-start | bytes 884744 | tf_op jit(solution)/shard_map/ppermute | solution.py:514
  129.7 8.4 %collective-permute-start.7 = (bf16[192,768]{1,0:T(8,128)(2,1)S(1)}, bf16[192,768]{1,0:T(8,128)(2,1)S(1)}, u32[]{:S(2)}, u32[]{:S(2)}) collective-permute-start(bf16[192,768]{1,0:T(8,128)(2,1)S(1)} %get-tuple-element.37), channel_id=1, source_target_pairs={{0,6},{2,4},{4,2},{6,0},{1,7},{3,5},{5,3},{7,1},{8,14},{10,12},{12... | collective-permute-start | bytes 884744 | tf_op jit(solution)/shard_map/ppermute | solution.py:514
  146.7 18.4 %all-to-all-start.6 = ((bf16[8,72,768]{2,1,0:T(8,128)(2,1)}), bf16[8,72,768]{2,1,0:T(8,128)(2,1)S(1)}, u32[]{:S(2)}, u32[]{:S(2)}) async-start(bf16[8,72,768]{2,1,0:T(8,128)(2,1)} %shard_map.142), calls=%async_computation.6 | async-start | bytes 1769472 | tf_op jit(solution)/shard_map/all_to_all | solution.py:508
  152.5 9.6 %collective-permute-start.8 = (bf16[192,768]{1,0:T(8,128)(2,1)}, bf16[192,768]{1,0:T(8,128)(2,1)}, u32[]{:S(2)}, u32[]{:S(2)}) collective-permute-start(bf16[192,768]{1,0:T(8,128)(2,1)} %copy-done.11), channel_id=1, source_target_pairs={{0,4},{2,6},{4,0},{6,2},{1,5},{3,7},{5,1},{7,3},{8,12},{10,14},{12... | collective-permute-start | bytes 884744 | tf_op jit(solution)/shard_map/ppermute | solution.py:514
  167.6 24.2 %all-to-all-start.7 = ((bf16[16,48,768]{2,1,0:T(8,128)(2,1)}), bf16[16,48,768]{2,1,0:T(8,128)(2,1)}, u32[]{:S(2)}, u32[]{:S(2)}) async-start(bf16[16,48,768]{2,1,0:T(8,128)(2,1)} %bitcast.21), calls=%async_computation.7 | async-start | bytes 2359296 | tf_op jit(solution)/shard_map/all_to_all | solution.py:508
  177.8 17.3 %collective-permute-start.9 = (bf16[48,1536]{1,0:T(8,128)(2,1)}, bf16[48,1536]{1,0:T(8,128)(2,1)S(1)}, u32[]{:S(2)}, u32[]{:S(2)}) collective-permute-start(bf16[48,1536]{1,0:T(8,128)(2,1)} %get-tuple-element.40), channel_id=1, source_target_pairs={{0,1},{1,0},{8,9},{9,8},{2,3},{3,2},{10,11},{11,10},{4,5},{5,4},{1... | collective-permute-start | bytes 442376 | tf_op jit(solution)/shard_map/ppermute | solution.py:514
  178.4 16.7 %collective-permute-start.10 = (bf16[48,1536]{1,0:T(8,128)(2,1)}, bf16[48,1536]{1,0:T(8,128)(2,1)S(1)}, u32[]{:S(2)}, u32[]{:S(2)}) collective-permute-start(bf16[48,1536]{1,0:T(8,128)(2,1)} %get-tuple-element.41), channel_id=1, source_target_pairs={{0,8},{1,9},{8,0},{9,1},{2,10},{3,11},{10,2},{11,3},{4,12},{5,13},... | collective-permute-start | bytes 442376 | tf_op jit(solution)/shard_map/ppermute | solution.py:514
  179.9 16.4 %collective-permute-start.11 = (bf16[48,1536]{1,0:T(8,128)(2,1)}, bf16[48,1536]{1,0:T(8,128)(2,1)S(1)}, u32[]{:S(2)}, u32[]{:S(2)}) collective-permute-start(bf16[48,1536]{1,0:T(8,128)(2,1)} %get-tuple-element.42), channel_id=1, source_target_pairs={{0,9},{1,8},{8,1},{9,0},{2,11},{3,10},{10,3},{11,2},{4,13},{5,12},... | collective-permute-start | bytes 442376 | tf_op jit(solution)/shard_map/ppermute | solution.py:514
  191.9 4.4 %copy-start.2 = (bf16[4,48,768]{2,1,0:T(8,128)(2,1)S(1)}, bf16[4,48,768]{2,1,0:T(8,128)(2,1)}, u32[]{:S(2)}) copy-start(bf16[4,48,768]{2,1,0:T(8,128)(2,1)} %x.7) | copy-start | bytes 884740
  191.9 4.4 %copy-start.3 = (bf16[768,768]{1,0:T(8,128)(2,1)S(1)}, bf16[768,768]{1,0:T(8,128)(2,1)}, u32[]{:S(2)}) copy-start(bf16[768,768]{1,0:T(8,128)(2,1)} %wq.5) | copy-start | bytes 3538948
  191.9 4.4 %copy-start.4 = (bf16[768,768]{1,0:T(8,128)(2,1)S(1)}, bf16[768,768]{1,0:T(8,128)(2,1)}, u32[]{:S(2)}) copy-start(bf16[768,768]{1,0:T(8,128)(2,1)} %wv.5) | copy-start | bytes 3538948
  191.9 4.4 %copy-start.9 = (f32[768]{0:T(1024)S(1)}, f32[768]{0:T(1024)}, u32[]{:S(2)}) copy-start(f32[768]{0:T(1024)} %gain.7) | copy-start | bytes 9220
where the time goes:
time: 200 us; the launch traced here: 199 us
  waiting for transfers between devices  65.3 us (33%)
  blocking collectives  48.2 us (24%)
  starting transfers between devices  43.7 us (22%)
  Pallas kernels  39.4 us (20%)
    all_to_all x3, blocking collectives, swap(): return lax.all_to_all(x, axes, split_axis=0, concat_axis=0, tiled=True)  48.2 us
    ppermute x12, waiting for transfers between devices, spread(): lax.ppermute(parts[k], axes, pairs[k])  44.5 us
    pallas_call x16, Pallas kernels, call(): pl.pallas_call(kernel, out_shape=shapes, in_specs=[pl.BlockSpec(memory_sp...  39.4 us
    all_to_all x5, starting transfers between devices, swap(): return lax.all_to_all(x, axes, split_axis=0, concat_axis=0, tiled=True)  30.4 us
    all_to_all x5, waiting for transfers between devices, swap(): return lax.all_to_all(x, axes, split_axis=0, concat_axis=0, tiled=True)  20.8 us
    ppermute x12, starting transfers between devices, spread(): lax.ppermute(parts[k], axes, pairs[k])  13.3 us
  transfers between devices with their start and end apart: 17, of which 12 were waited for; matrix products, arithmetic and copies ran while one was open for 0% of the time, Pallas kernels for 7%

commit v1 on v0

--- a/solution.py
+++ b/solution.py
@@ -28,6 +28,7 @@
 ROWS = GH * I // NS
 SENT = S * CR
 BLOCK = ROWS + 2 * SENT
+READ = 80
 WIDTH = GH * S * HEAD_DIM
 ROW_SCALE = 1.0 / math.sqrt(HEAD_DIM * 32)
 COL_SCALE = 1.0 / math.sqrt(HEAD_DIM)
@@ -250,9 +251,9 @@
 
 
 def summed(parts):
-    total = parts[0].astype(F32)
+    total = parts[0, 0:READ].astype(F32)
     for a in range(1, NS):
-        total = total + parts[a].astype(F32)
+        total = total + parts[a, 0:READ].astype(F32)
     return total[:ROWS]
 
 

time: 200 us -> 200 us (level)
  no operation moved by 1% of the time
where the time goes in v1:
time: 200 us; the launch traced here: 199 us
  waiting for transfers between devices  65.3 us (33%)
  blocking collectives  48.2 us (24%)
  starting transfers between devices  43.7 us (22%)
  Pallas kernels  39.4 us (20%)
    all_to_all x3, blocking collectives, swap(): return lax.all_to_all(x, axes, split_axis=0, concat_axis=0, tiled=True)  48.2 us
    ppermute x12, waiting for transfers between devices, spread(): lax.ppermute(parts[k], axes, pairs[k])  44.5 us
    pallas_call x16, Pallas kernels, call(): pl.pallas_call(kernel, out_shape=shapes, in_specs=[pl.BlockSpec(memory_sp...  39.4 us
    all_to_all x5, starting transfers between devices, swap(): return lax.all_to_all(x, axes, split_axis=0, concat_axis=0, tiled=True)  30.4 us
    all_to_all x5, waiting for transfers between devices, swap(): return lax.all_to_all(x, axes, split_axis=0, concat_axis=0, tiled=True)  20.8 us
    ppermute x12, starting transfers between devices, spread(): lax.ppermute(parts[k], axes, pairs[k])  13.3 us
  transfers between devices with their start and end apart: 17, of which 12 were waited for; matrix products, arithmetic and copies ran while one was open for 0% of the time, Pallas kernels for 7%

profile of v1, /device:TPU:1, one launch (start us, length us, event | category | flops | bytes accessed | tf_op | source)
XLA Modules:
  0.0 199.4 jit_solution(7637418864967703055)
XLA Ops:
  0.6 2.9 %shard_map.132 = bf16[16,48,768]{2,1,0:T(8,128)(2,1)} custom-call(bf16[4,48,768]{2,1,0:T(8,128)(2,1)} %x.7, f32[768]{0:T(1024)} %gain.7, bf16[768,768]{1,0:T(8,128)(2,1)} %wk.3), custom_call_target="tpu_custom_call" | custom-call | tf_op jit(solution)/shard_map/pallas_call | solution.py:59
  3.6 6.9 %all-to-all-start = ((bf16[16,48,768]{2,1,0:T(8,128)(2,1)}), bf16[16,48,768]{2,1,0:T(8,128)(2,1)S(1)}, u32[]{:S(2)}, u32[]{:S(2)}) async-start(bf16[16,48,768]{2,1,0:T(8,128)(2,1)} %shard_map.132), calls=%async_computation | async-start | bytes 2359296 | tf_op jit(solution)/shard_map/all_to_all | solution.py:509
  10.5 2.6 %shard_map.131 = (bf16[48,1536]{1,0:T(8,128)(2,1)S(1)}, bf16[48,1536]{1,0:T(8,128)(2,1)S(1)}, bf16[48,1536]{1,0:T(8,128)(2,1)S(1)}, bf16[48,1536]{1,0:T(8,128)(2,1)S(1)}) custom-call(bf16[4,48,768]{2,1,0:T(8,128)(2,1)} %x.7, f32[768]{0:T(1024)} %gain.7, bf16[768,768]{1,0:T(8,128)(2,1)} %wq.5, bf16[768,768]{1,0:T(8,128)(2,1)} %wv.5), custom_call_target="tpu_custom_call" | custom-call | tf_op jit(solution)/shard_map/pallas_call | solution.py:59
  15.4 13.7 %collective-permute-done.1.qv2 = bf16[48,1536]{1,0:T(8,128)(2,1)S(1)} collective-permute-done((bf16[48,1536]{1,0:T(8,128)(2,1)S(1)}, bf16[48,1536]{1,0:T(8,128)(2,1)S(1)}, u32[]{:S(2)}, u32[]{:S(2)}) %collective-permute-start.1) | collective-permute-done | bytes 147488 | tf_op jit(solution)/shard_map/ppermute | solution.py:515
  29.0 3.3 %collective-permute-done.2.qv3 = bf16[48,1536]{1,0:T(8,128)(2,1)S(1)} collective-permute-done((bf16[48,1536]{1,0:T(8,128)(2,1)S(1)}, bf16[48,1536]{1,0:T(8,128)(2,1)S(1)}, u32[]{:S(2)}, u32[]{:S(2)}) %collective-permute-start.2) | collective-permute-done | bytes 147488 | tf_op jit(solution)/shard_map/ppermute | solution.py:515
  32.4 1.7 shard_map.133
  34.1 7.3 %all-to-all-start.1 = ((bf16[8,120,768]{2,1,0:T(8,128)(2,1)}), bf16[8,120,768]{2,1,0:T(8,128)(2,1)S(1)}, u32[]{:S(2)}, u32[]{:S(2)}) async-start(bf16[8,120,768]{2,1,0:T(8,128)(2,1)} %get-tuple-element.27), calls=%async_computation.1 | async-start | bytes 2949120 | tf_op jit(solution)/shard_map/all_to_all | solution.py:509
  41.4 2.3 %collective-permute-start.5 = (bf16[192,768]{1,0:T(8,128)(2,1)S(1)}, bf16[192,768]{1,0:T(8,128)(2,1)S(1)}, u32[]{:S(2)}, u32[]{:S(2)}) collective-permute-start(bf16[192,768]{1,0:T(8,128)(2,1)S(1)} %bitcast.23), channel_id=1, source_target_pairs={{0,6},{2,4},{4,2},{6,0},{1,7},{3,5},{5,3},{7,1},{8,14},{10,12},{12... | collective-permute-start | bytes 884744 | tf_op jit(solution)/shard_map/ppermute | solution.py:515
  44.8 12.4 %collective-permute-done.5.v3 = bf16[192,768]{1,0:T(8,128)(2,1)S(1)} collective-permute-done((bf16[192,768]{1,0:T(8,128)(2,1)S(1)}, bf16[192,768]{1,0:T(8,128)(2,1)S(1)}, u32[]{:S(2)}, u32[]{:S(2)}) %collective-permute-start.5) | collective-permute-done | bytes 294944 | tf_op jit(solution)/shard_map/ppermute | solution.py:515
  57.5 2.0 %shard_map.134.values = bf16[4,192,768]{2,1,0:T(8,128)(2,1)} custom-call(bf16[192,768]{1,0:T(8,128)(2,1)} %bitcast.22, bf16[192,768]{1,0:T(8,128)(2,1)S(1)} %collective-permute-done.3.v1, bf16[192,768]{1,0:T(8,128)(2,1)S(1)} %collective-permute-done.4.v2, bf16[192,768]{1,0:T(8,128)(2,1)S(1)} %collective-permute-done.5.v3), custom_call_target="tpu_custom_call" | custom-call | tf_op jit(solution)/shard_map/pallas_call | solution.py:59
  62.0 18.5 %all_to_all.58 = bf16[8,72,768]{2,1,0:T(8,128)(2,1)S(1)} all-to-all(bf16[8,72,768]{2,1,0:T(8,128)(2,1)S(1)} %get-tuple-element.29), channel_id=1, replica_groups=mesh['xh'=2,'z'=4,'xl'=2,'y'=4,'c'=2] {'xh','z'}, dimensions={0} | all-to-all | bytes 1769472 | tf_op jit(solution)/shard_map/all_to_all | solution.py:509
  81.5 15.6 %all_to_all.59 = bf16[32,8,768]{2,1,0:T(8,128)(2,1)S(1)} all-to-all(bf16[32,8,768]{2,1,0:T(8,128)(2,1)S(1)} %bitcast.18), channel_id=1, replica_groups=mesh['xh'=2,'z'=4,'xl'=2,'y'=4,'c'=2] {'xh','z','xl','c'}, dimensions={0} | all-to-all | bytes 786432 | tf_op jit(solution)/shard_map/all_to_all | solution.py:509
  97.2 9.3 %shard_map.137 = (bf16[192,1536]{1,0:T(8,128)(2,1)S(1)}, bf16[256,768]{1,0:T(8,128)(2,1)S(1)}) custom-call(bf16[256,768]{1,0:T(8,128)(2,1)S(1)} %bitcast.17, bf16[8,120,768]{2,1,0:T(8,128)(2,1)S(1)} %all-to-all-done.1.parts.sent, f32[768]{0:T(1024)S(1)} %copy-done.10, bf16[768,768]{1,0:T(8,128)(2,1)S(1)} %copy-done.5, bf16[768,768]{1,0:T(8,128)(2,1)S(1)} %copy-done.6, ...), custom_call_target="tpu_custom_call" | custom-call | tf_op jit(solution)/shard_map/pallas_call | solution.py:59
  106.5 14.1 %all_to_all.60 = bf16[32,8,768]{2,1,0:T(8,128)(2,1)S(1)} all-to-all(bf16[32,8,768]{2,1,0:T(8,128)(2,1)S(1)} %bitcast.20), channel_id=1, replica_groups=mesh['xh'=2,'z'=4,'xl'=2,'y'=4,'c'=2] {'xh','z','xl','c'}, dimensions={0} | all-to-all | bytes 786432 | tf_op jit(solution)/shard_map/all_to_all | solution.py:509
  120.6 1.7 shard_map.138
  122.2 3.6 %all-to-all-start.5 = ((bf16[8,120,768]{2,1,0:T(8,128)(2,1)}), bf16[8,120,768]{2,1,0:T(8,128)(2,1)S(1)}, u32[]{:S(2)}, u32[]{:S(2)}) async-start(bf16[8,120,768]{2,1,0:T(8,128)(2,1)} %get-tuple-element.32), calls=%async_computation.5 | async-start | bytes 2949120 | tf_op jit(solution)/shard_map/all_to_all | solution.py:509
  129.7 1.9 collective-permute-start.7
  131.6 4.7 %collective-permute-done.6.gv1 = bf16[192,768]{1,0:T(8,128)(2,1)S(1)} collective-permute-done((bf16[192,768]{1,0:T(8,128)(2,1)S(1)}, bf16[192,768]{1,0:T(8,128)(2,1)S(1)}, u32[]{:S(2)}, u32[]{:S(2)}) %collective-permute-start.6) | collective-permute-done | bytes 294944 | tf_op jit(solution)/shard_map/ppermute | solution.py:515
  136.2 1.9 collective-permute-done.7.gv3
  138.1 1.8 shard_map.141.gv
  140.0 4.7 %all-to-all-done.5.sent.parts = bf16[8,120,768]{2,1,0:T(8,128)(2,1)S(1)} async-done(((bf16[8,120,768]{2,1,0:T(8,128)(2,1)}), bf16[8,120,768]{2,1,0:T(8,128)(2,1)S(1)}, u32[]{:S(2)}, u32[]{:S(2)}) %all-to-all-start.5) | async-done | bytes 1474592 | tf_op jit(solution)/shard_map/all_to_all | solution.py:509
  144.7 2.1 %shard_map.142 = bf16[8,72,768]{2,1,0:T(8,128)(2,1)} custom-call(bf16[8,120,768]{2,1,0:T(8,128)(2,1)S(1)} %all-to-all-done.5.sent.parts, f32[72,768]{1,0:T(8,128)} %get-tuple-element.33.probs, f32[192,768]{1,0:T(8,128)} %shard_map.141.gv), custom_call_target="tpu_custom_call" | custom-call | tf_op jit(solution)/shard_map/pallas_call | solution.py:59
  146.7 5.8 %all-to-all-start.6 = ((bf16[8,72,768]{2,1,0:T(8,128)(2,1)}), bf16[8,72,768]{2,1,0:T(8,128)(2,1)S(1)}, u32[]{:S(2)}, u32[]{:S(2)}) async-start(bf16[8,72,768]{2,1,0:T(8,128)(2,1)} %shard_map.142), calls=%async_computation.6 | async-start | bytes 1769472 | tf_op jit(solution)/shard_map/all_to_all | solution.py:509
  152.5 2.5 %collective-permute-start.8 = (bf16[192,768]{1,0:T(8,128)(2,1)}, bf16[192,768]{1,0:T(8,128)(2,1)}, u32[]{:S(2)}, u32[]{:S(2)}) collective-permute-start(bf16[192,768]{1,0:T(8,128)(2,1)} %copy-done.11), channel_id=1, source_target_pairs={{0,4},{2,6},{4,0},{6,2},{1,5},{3,7},{5,1},{7,3},{8,12},{10,14},{12... | collective-permute-start | bytes 884744 | tf_op jit(solution)/shard_map/ppermute | solution.py:515
  155.0 7.1 %collective-permute-done.8.gv2.before = bf16[192,768]{1,0:T(8,128)(2,1)} collective-permute-done((bf16[192,768]{1,0:T(8,128)(2,1)}, bf16[192,768]{1,0:T(8,128)(2,1)}, u32[]{:S(2)}, u32[]{:S(2)}) %collective-permute-start.8) | collective-permute-done | bytes 294944 | tf_op jit(solution)/shard_map/ppermute | solution.py:515
  162.1 3.0 %all-to-all-done.6 = bf16[8,72,768]{2,1,0:T(8,128)(2,1)S(1)} async-done(((bf16[8,72,768]{2,1,0:T(8,128)(2,1)}), bf16[8,72,768]{2,1,0:T(8,128)(2,1)S(1)}, u32[]{:S(2)}, u32[]{:S(2)}) %all-to-all-start.6) | async-done | bytes 884768 | tf_op jit(solution)/shard_map/all_to_all | solution.py:509
  165.1 2.5 %shard_map.144 = bf16[768,768]{1,0:T(8,128)(2,1)} custom-call(bf16[576,768]{1,0:T(8,128)(2,1)S(1)} %bitcast.15, bf16[192,768]{1,0:T(8,128)(2,1)} %bitcast.26, bf16[192,768]{1,0:T(8,128)(2,1)} %collective-permute-done.8.gv2.before), custom_call_target="tpu_custom_call" | custom-call | tf_op jit(solution)/shard_map/pallas_call | solution.py:59
  167.6 6.8 %all-to-all-start.7 = ((bf16[16,48,768]{2,1,0:T(8,128)(2,1)}), bf16[16,48,768]{2,1,0:T(8,128)(2,1)}, u32[]{:S(2)}, u32[]{:S(2)}) async-start(bf16[16,48,768]{2,1,0:T(8,128)(2,1)} %bitcast.21), calls=%async_computation.7 | async-start | bytes 2359296 | tf_op jit(solution)/shard_map/all_to_all | solution.py:509
  175.4 2.4 %shard_map.143 = (bf16[48,1536]{1,0:T(8,128)(2,1)}, bf16[48,1536]{1,0:T(8,128)(2,1)}, bf16[48,1536]{1,0:T(8,128)(2,1)}, bf16[48,1536]{1,0:T(8,128)(2,1)}) custom-call(bf16[576,768]{1,0:T(8,128)(2,1)S(1)} %bitcast.16, bf16[768,768]{1,0:T(8,128)(2,1)S(1)} %bitcast.12, f32[192,768]{1,0:T(8,128)} %shard_map.141.gv, ...), custom_call_target="tpu_custom_call" | custom-call | tf_op jit(solution)/shard_map/pallas_call | solution.py:59
  180.2 11.6 %all-to-all-done.7 = bf16[16,48,768]{2,1,0:T(8,128)(2,1)} async-done(((bf16[16,48,768]{2,1,0:T(8,128)(2,1)}), bf16[16,48,768]{2,1,0:T(8,128)(2,1)}, u32[]{:S(2)}, u32[]{:S(2)}) %all-to-all-start.7) | async-done | bytes 1179680 | tf_op jit(solution)/shard_map/all_to_all | solution.py:509
  191.9 3.2 %shard_map.145.part = f32[192,768]{1,0:T(8,128)} custom-call(bf16[768,768]{1,0:T(8,128)(2,1)} %bitcast.10.gk, bf16[768,768]{1,0:T(8,128)(2,1)} %wk.3), custom_call_target="tpu_custom_call" | custom-call | flops 4000000000 | bytes 3000000 | tf_op jit(solution)/shard_map/pallas_call | solution.py:59
  196.3 2.9 %shard_map.146 = bf16[4,48,768]{2,1,0:T(8,128)(2,1)} custom-call(bf16[48,1536]{1,0:T(8,128)(2,1)} %get-tuple-element.39.gqv0, bf16[48,1536]{1,0:T(8,128)(2,1)S(1)} %collective-permute-done.9.gqv1, bf16[48,1536]{1,0:T(8,128)(2,1)S(1)} %collective-permute-done.10.gqv2, bf16[48,1536]{1,0:T(8,128)(2,1)S(1)} %collective-permute-done.11.gqv3, ...), custom_call_target="tpu_custom_call" | custom-call | tf_op jit(solution)/shard_map/pallas_call | solution.py:59
  (47 shorter events, 15.7 us)
Async XLA Ops:
  3.6 28.8 %all-to-all-start = ((bf16[16,48,768]{2,1,0:T(8,128)(2,1)}), bf16[16,48,768]{2,1,0:T(8,128)(2,1)S(1)}, u32[]{:S(2)}, u32[]{:S(2)}) async-start(bf16[16,48,768]{2,1,0:T(8,128)(2,1)} %shard_map.132), calls=%async_computation | async-start | bytes 2359296 | tf_op jit(solution)/shard_map/all_to_all | solution.py:509
  10.5 21.9 %copy-start.1 = (bf16[4,48,768]{2,1,0:T(8,128)(2,1)S(1)}, bf16[4,48,768]{2,1,0:T(8,128)(2,1)}, u32[]{:S(2)}) copy-start(bf16[4,48,768]{2,1,0:T(8,128)(2,1)} %x.7) | copy-start | bytes 884740
  10.5 21.9 %copy-start.7 = (bf16[4,48,768]{2,1,0:T(8,128)(2,1)S(1)}, bf16[4,48,768]{2,1,0:T(8,128)(2,1)}, u32[]{:S(2)}) copy-start(bf16[4,48,768]{2,1,0:T(8,128)(2,1)} %cot.1) | copy-start | bytes 884740
  13.1 2.2 %collective-permute-start = (bf16[48,1536]{1,0:T(8,128)(2,1)S(1)}, bf16[48,1536]{1,0:T(8,128)(2,1)S(1)}, u32[]{:S(2)}, u32[]{:S(2)}) collective-permute-start(bf16[48,1536]{1,0:T(8,128)(2,1)S(1)} %get-tuple-element.24), channel_id=1, source_target_pairs={{0,1},{1,0},{8,9},{9,8},{2,3},{3,2},{10,11},{11,10},{4,5},{5,4},{1... | collective-permute-start | bytes 442376 | tf_op jit(solution)/shard_map/ppermute | solution.py:515
  13.3 15.7 %collective-permute-start.1 = (bf16[48,1536]{1,0:T(8,128)(2,1)S(1)}, bf16[48,1536]{1,0:T(8,128)(2,1)S(1)}, u32[]{:S(2)}, u32[]{:S(2)}) collective-permute-start(bf16[48,1536]{1,0:T(8,128)(2,1)S(1)} %get-tuple-element.25), channel_id=1, source_target_pairs={{0,8},{1,9},{8,0},{9,1},{2,10},{3,11},{10,2},{11,3},{4,12},{5,13},... | collective-permute-start | bytes 442376 | tf_op jit(solution)/shard_map/ppermute | solution.py:515
  15.0 17.4 %collective-permute-start.2 = (bf16[48,1536]{1,0:T(8,128)(2,1)S(1)}, bf16[48,1536]{1,0:T(8,128)(2,1)S(1)}, u32[]{:S(2)}, u32[]{:S(2)}) collective-permute-start(bf16[48,1536]{1,0:T(8,128)(2,1)S(1)} %get-tuple-element.26), channel_id=1, source_target_pairs={{0,9},{1,8},{8,1},{9,0},{2,11},{3,10},{10,3},{11,2},{4,13},{5,12},... | collective-permute-start | bytes 442376 | tf_op jit(solution)/shard_map/ppermute | solution.py:515
  34.1 7.4 %copy-start.12 = (bf16[4,48,768]{2,1,0:T(8,128)(2,1)S(1)}, bf16[4,48,768]{2,1,0:T(8,128)(2,1)}, u32[]{:S(2)}) copy-start(bf16[4,48,768]{2,1,0:T(8,128)(2,1)} %get-tuple-element.28) | copy-start | bytes 884740
  34.1 26.9 %all-to-all-start.1 = ((bf16[8,120,768]{2,1,0:T(8,128)(2,1)}), bf16[8,120,768]{2,1,0:T(8,128)(2,1)S(1)}, u32[]{:S(2)}, u32[]{:S(2)}) async-start(bf16[8,120,768]{2,1,0:T(8,128)(2,1)} %get-tuple-element.27), calls=%async_computation.1 | async-start | bytes 2949120 | tf_op jit(solution)/shard_map/all_to_all | solution.py:509
  41.4 15.7 %collective-permute-start.5 = (bf16[192,768]{1,0:T(8,128)(2,1)S(1)}, bf16[192,768]{1,0:T(8,128)(2,1)S(1)}, u32[]{:S(2)}, u32[]{:S(2)}) collective-permute-start(bf16[192,768]{1,0:T(8,128)(2,1)S(1)} %bitcast.23), channel_id=1, source_target_pairs={{0,6},{2,4},{4,2},{6,0},{1,7},{3,5},{5,3},{7,1},{8,14},{10,12},{12... | collective-permute-start | bytes 884744 | tf_op jit(solution)/shard_map/ppermute | solution.py:515
  43.7 13.4 %collective-permute-start.4 = (bf16[192,768]{1,0:T(8,128)(2,1)S(1)}, bf16[192,768]{1,0:T(8,128)(2,1)S(1)}, u32[]{:S(2)}, u32[]{:S(2)}) collective-permute-start(bf16[192,768]{1,0:T(8,128)(2,1)S(1)} %bitcast.24), channel_id=1, source_target_pairs={{0,4},{2,6},{4,0},{6,2},{1,5},{3,7},{5,1},{7,3},{8,12},{10,14},{12... | collective-permute-start | bytes 884744 | tf_op jit(solution)/shard_map/ppermute | solution.py:515
  44.2 13.2 %collective-permute-start.3 = (bf16[192,768]{1,0:T(8,128)(2,1)S(1)}, bf16[192,768]{1,0:T(8,128)(2,1)S(1)}, u32[]{:S(2)}, u32[]{:S(2)}) collective-permute-start(bf16[192,768]{1,0:T(8,128)(2,1)S(1)} %bitcast.25), channel_id=1, source_target_pairs={{0,2},{2,0},{4,6},{6,4},{1,3},{3,1},{5,7},{7,5},{8,10},{10,8},{12,... | collective-permute-start | bytes 884744 | tf_op jit(solution)/shard_map/ppermute | solution.py:515
  62.0 18.5 %copy-start = (bf16[4,192,768]{2,1,0:T(8,128)(2,1)S(1)}, bf16[4,192,768]{2,1,0:T(8,128)(2,1)}, u32[]{:S(2)}) copy-start(bf16[4,192,768]{2,1,0:T(8,128)(2,1)} %shard_map.134.values) | copy-start | bytes 3538948
  80.4 16.7 %copy-start.5 = (bf16[768,768]{1,0:T(8,128)(2,1)S(1)}, bf16[768,768]{1,0:T(8,128)(2,1)}, u32[]{:S(2)}) copy-start(bf16[768,768]{1,0:T(8,128)(2,1)} %out_row.1) | copy-start | bytes 3538948
  80.4 16.7 %copy-start.6 = (bf16[768,768]{1,0:T(8,128)(2,1)S(1)}, bf16[768,768]{1,0:T(8,128)(2,1)}, u32[]{:S(2)}) copy-start(bf16[768,768]{1,0:T(8,128)(2,1)} %wq.4) | copy-start | bytes 3538948
  80.4 16.7 %copy-start.10 = (f32[768]{0:T(1024)S(1)}, f32[768]{0:T(1024)}, u32[]{:S(2)}) copy-start(f32[768]{0:T(1024)} %gain.6) | copy-start | bytes 9220
  122.2 22.4 %all-to-all-start.5 = ((bf16[8,120,768]{2,1,0:T(8,128)(2,1)}), bf16[8,120,768]{2,1,0:T(8,128)(2,1)S(1)}, u32[]{:S(2)}, u32[]{:S(2)}) async-start(bf16[8,120,768]{2,1,0:T(8,128)(2,1)} %get-tuple-element.32), calls=%async_computation.5 | async-start | bytes 2949120 | tf_op jit(solution)/shard_map/all_to_all | solution.py:509
  125.8 1.0 copy-start.8
  128.1 0.7 copy-start.11
  128.8 7.5 %collective-permute-start.6 = (bf16[192,768]{1,0:T(8,128)(2,1)S(1)}, bf16[192,768]{1,0:T(8,128)(2,1)S(1)}, u32[]{:S(2)}, u32[]{:S(2)}) collective-permute-start(bf16[192,768]{1,0:T(8,128)(2,1)S(1)} %get-tuple-element.36), channel_id=1, source_target_pairs={{0,2},{2,0},{4,6},{6,4},{1,3},{3,1},{5,7},{7,5},{8,10},{10,8},{12,... | collective-permute-start | bytes 884744 | tf_op jit(solution)/shard_map/ppermute | solution.py:515
  129.7 8.4 %collective-permute-start.7 = (bf16[192,768]{1,0:T(8,128)(2,1)S(1)}, bf16[192,768]{1,0:T(8,128)(2,1)S(1)}, u32[]{:S(2)}, u32[]{:S(2)}) collective-permute-start(bf16[192,768]{1,0:T(8,128)(2,1)S(1)} %get-tuple-element.37), channel_id=1, source_target_pairs={{0,6},{2,4},{4,2},{6,0},{1,7},{3,5},{5,3},{7,1},{8,14},{10,12},{12... | collective-permute-start | bytes 884744 | tf_op jit(solution)/shard_map/ppermute | solution.py:515
  146.7 18.4 %all-to-all-start.6 = ((bf16[8,72,768]{2,1,0:T(8,128)(2,1)}), bf16[8,72,768]{2,1,0:T(8,128)(2,1)S(1)}, u32[]{:S(2)}, u32[]{:S(2)}) async-start(bf16[8,72,768]{2,1,0:T(8,128)(2,1)} %shard_map.142), calls=%async_computation.6 | async-start | bytes 1769472 | tf_op jit(solution)/shard_map/all_to_all | solution.py:509
  152.5 9.6 %collective-permute-start.8 = (bf16[192,768]{1,0:T(8,128)(2,1)}, bf16[192,768]{1,0:T(8,128)(2,1)}, u32[]{:S(2)}, u32[]{:S(2)}) collective-permute-start(bf16[192,768]{1,0:T(8,128)(2,1)} %copy-done.11), channel_id=1, source_target_pairs={{0,4},{2,6},{4,0},{6,2},{1,5},{3,7},{5,1},{7,3},{8,12},{10,14},{12... | collective-permute-start | bytes 884744 | tf_op jit(solution)/shard_map/ppermute | solution.py:515
  167.6 24.2 %all-to-all-start.7 = ((bf16[16,48,768]{2,1,0:T(8,128)(2,1)}), bf16[16,48,768]{2,1,0:T(8,128)(2,1)}, u32[]{:S(2)}, u32[]{:S(2)}) async-start(bf16[16,48,768]{2,1,0:T(8,128)(2,1)} %bitcast.21), calls=%async_computation.7 | async-start | bytes 2359296 | tf_op jit(solution)/shard_map/all_to_all | solution.py:509
  177.8 17.3 %collective-permute-start.9 = (bf16[48,1536]{1,0:T(8,128)(2,1)}, bf16[48,1536]{1,0:T(8,128)(2,1)S(1)}, u32[]{:S(2)}, u32[]{:S(2)}) collective-permute-start(bf16[48,1536]{1,0:T(8,128)(2,1)} %get-tuple-element.40), channel_id=1, source_target_pairs={{0,1},{1,0},{8,9},{9,8},{2,3},{3,2},{10,11},{11,10},{4,5},{5,4},{1... | collective-permute-start | bytes 442376 | tf_op jit(solution)/shard_map/ppermute | solution.py:515
  178.4 16.7 %collective-permute-start.10 = (bf16[48,1536]{1,0:T(8,128)(2,1)}, bf16[48,1536]{1,0:T(8,128)(2,1)S(1)}, u32[]{:S(2)}, u32[]{:S(2)}) collective-permute-start(bf16[48,1536]{1,0:T(8,128)(2,1)} %get-tuple-element.41), channel_id=1, source_target_pairs={{0,8},{1,9},{8,0},{9,1},{2,10},{3,11},{10,2},{11,3},{4,12},{5,13},... | collective-permute-start | bytes 442376 | tf_op jit(solution)/shard_map/ppermute | solution.py:515
  179.9 16.4 %collective-permute-start.11 = (bf16[48,1536]{1,0:T(8,128)(2,1)}, bf16[48,1536]{1,0:T(8,128)(2,1)S(1)}, u32[]{:S(2)}, u32[]{:S(2)}) collective-permute-start(bf16[48,1536]{1,0:T(8,128)(2,1)} %get-tuple-element.42), channel_id=1, source_target_pairs={{0,9},{1,8},{8,1},{9,0},{2,11},{3,10},{10,3},{11,2},{4,13},{5,12},... | collective-permute-start | bytes 442376 | tf_op jit(solution)/shard_map/ppermute | solution.py:515
  191.9 4.4 %copy-start.2 = (bf16[4,48,768]{2,1,0:T(8,128)(2,1)S(1)}, bf16[4,48,768]{2,1,0:T(8,128)(2,1)}, u32[]{:S(2)}) copy-start(bf16[4,48,768]{2,1,0:T(8,128)(2,1)} %x.7) | copy-start | bytes 884740
  191.9 4.4 %copy-start.3 = (bf16[768,768]{1,0:T(8,128)(2,1)S(1)}, bf16[768,768]{1,0:T(8,128)(2,1)}, u32[]{:S(2)}) copy-start(bf16[768,768]{1,0:T(8,128)(2,1)} %wq.5) | copy-start | bytes 3538948
  191.9 4.4 %copy-start.4 = (bf16[768,768]{1,0:T(8,128)(2,1)S(1)}, bf16[768,768]{1,0:T(8,128)(2,1)}, u32[]{:S(2)}) copy-start(bf16[768,768]{1,0:T(8,128)(2,1)} %wv.5) | copy-start | bytes 3538948
  191.9 4.4 %copy-start.9 = (f32[768]{0:T(1024)S(1)}, f32[768]{0:T(1024)}, u32[]{:S(2)}) copy-start(f32[768]{0:T(1024)} %gain.7) | copy-start | bytes 9220
